TPU v7x, 32 devices: a whole 2x2x4 slice. The times are simulated.
32 devices in a mesh: dp: 32 (over z, y, x, core).
Axes of the slice: x: 2, y: 2, z: 4, core: 2. Of those that a mesh axis runs over, the one named last changes fastest.
Arguments:
- tokens: bfloat16 [32, 1024, 512], P('dp'), may hold values from -6 to 6
- memory: bfloat16 [32, 1024, 512], P('dp'), may hold values from -6 to 6
- directions: int32 [32], P('dp'), may hold values from 0 to 1
- target_len: int32 [32], P('dp'), may hold values from 256 to 1024, as said below
- memory_len: int32 [32], P('dp'), may hold values from 256 to 1024, as said below
- self_qkv: bfloat16 [786432], P('dp'), may hold values from -0.25 to 0.25
- self_out: bfloat16 [262144], P('dp'), may hold values from -1 to 1
- cross_query: bfloat16 [262144], P('dp'), may hold values from -0.25 to 0.25
- cross_kv: bfloat16 [524288], P('dp'), may hold values from -0.25 to 0.25
- cross_out: bfloat16 [262144], P('dp'), may hold values from -1 to 1
- ffn_in: bfloat16 [1048576], P('dp'), may hold values from -0.25 to 0.25
- ffn_out: bfloat16 [1048576], P('dp'), may hold values from -0.125 to 0.125
- vectors: bfloat16 [9728], P('dp'), may hold values from -1.2 to 1.6
- cotangent: bfloat16 [32, 1024, 512], P('dp'), may hold values from -6 to 6
Outputs:
- out: bfloat16 [32, 1024, 512], P('dp')
- d_tokens: float32 [32, 1024, 512], P('dp')
- d_memory: float32 [32, 1024, 512], P('dp')
- g_self_qkv: float32 [786432], P('dp')
- g_self_out: float32 [262144], P('dp')
- g_cross_query: float32 [262144], P('dp')
- g_cross_kv: float32 [524288], P('dp')
- g_cross_out: float32 [262144], P('dp')
- g_ffn_in: float32 [1048576], P('dp')
- g_ffn_out: float32 [1048576], P('dp')
- g_vectors: float32 [9728], P('dp')
Inputs may be any that keep to these rules, and one draw needn't show every extreme that they name: `target_len`: positions from this length on are padding; some sequence has exactly 1024 and some exactly 256. `memory_len`: memory positions from this length on are padding; some sequence has exactly 1024 and some exactly 256.
All inputs are finite; a program needn't handle non-finite values.
Results may differ from a plain program's by a relative error of at most 0.017.
The roundings to bfloat16 on the way count: a program that leaves them out, or rounds other values in their place, can miss the bound.
Values may be sent and summed in bfloat16 or wider, within the bound.
No kernel may reach another device: no remote copies, remote signals or barrier semaphores. Data moves between devices by JAX's collectives and lax.ppermute only.
A program may use at most 128 MiB of HBM per device.

v0:
```python
import jax
import jax.numpy as jnp
from jax import lax
from jax.sharding import PartitionSpec as P

HEADS = 8


mask_fill = -1000000000.0
norm_eps = 1e-05


def to_low(values):
    return values.astype(jnp.bfloat16)


def product(left, right):
    return jnp.dot(left, right, preferred_element_type=jnp.float32)


def outer_sum(left, right):
    return lax.dot_general(
        left, right, (((0,), (0,)), ((), ())), preferred_element_type=jnp.float32
    )


def back_product(left, right):
    return lax.dot_general(
        left, right, (((1,), (1,)), ((), ())), preferred_element_type=jnp.float32
    )


def norm_layer(values, gain, shift):
    center = jnp.mean(values, axis=-1, keepdims=True)
    offsets = values - center
    spread = jnp.mean(offsets * offsets, axis=-1, keepdims=True)
    return offsets * lax.rsqrt(spread + norm_eps) * gain + shift


def gelu_exact(values):
    return jax.nn.gelu(values, approximate=False)


def head_pairs(matrix, pair_id, pair_width):
    sliced = lax.dynamic_slice_in_dim(matrix, pair_id * pair_width, pair_width, 1)
    return sliced.reshape(matrix.shape[0], 2, pair_width // 2)


def allowed_block(offset, block_rows, key_count, key_limit, causal):
    query_pos = offset + lax.iota(jnp.int32, block_rows)
    key_pos = lax.iota(jnp.int32, key_count)
    if causal:
        return key_pos[None, :] <= query_pos[:, None]
    return jnp.broadcast_to((key_pos < key_limit)[None, :], (block_rows, key_count))


def score_block(query_block, key_heads, allowed, score_scale):
    scores = (
        jnp.einsum("qhd,khd->hqk", query_block, key_heads, preferred_element_type=jnp.float32)
        * score_scale
    )
    return jnp.where(allowed[None], scores, mask_fill)


def attend_forward(queries, key_rows, value_rows, key_limit, causal):
    length, model_width = queries.shape
    key_count = key_rows.shape[0]
    head_dim = model_width // HEADS
    pair_width = 2 * head_dim
    score_scale = head_dim ** (-0.5)
    block_rows = min(512, length)

    def one_group(pair_id):
        query_heads = head_pairs(queries, pair_id, pair_width)
        key_heads = head_pairs(key_rows, pair_id, pair_width)
        value_heads = head_pairs(value_rows, pair_id, pair_width)

        def one_block(block_id):
            offset = block_id * block_rows
            query_block = lax.dynamic_slice_in_dim(query_heads, offset, block_rows, 0)
            allowed = allowed_block(offset, block_rows, key_count, key_limit, causal)
            scores = score_block(query_block, key_heads, allowed, score_scale)
            highest = jnp.max(scores, axis=-1, keepdims=True)
            powered = jnp.exp(scores - highest)
            totals = jnp.sum(powered, axis=-1, keepdims=True)
            chances = to_low(powered / totals)
            blended = jnp.einsum(
                "hqk,khd->qhd", chances, value_heads, preferred_element_type=jnp.float32
            )
            return (blended.reshape(block_rows, pair_width), (highest + jnp.log(totals))[..., 0])

        blended, log_sums = lax.map(one_block, jnp.arange(length // block_rows))
        return (blended.reshape(length, pair_width), log_sums)

    blended, log_sums = lax.map(one_group, jnp.arange(model_width // pair_width))
    return (blended.transpose(1, 0, 2).reshape(length, model_width), log_sums)


def attend_backward(queries, key_rows, value_rows, log_sums, grad_out, key_limit, causal):
    length, model_width = queries.shape
    key_count = key_rows.shape[0]
    head_dim = model_width // HEADS
    pair_width = 2 * head_dim
    score_scale = head_dim ** (-0.5)
    block_rows = min(512, length)

    def one_group(inputs):
        pair_id, group_sums = inputs
        query_heads = head_pairs(queries, pair_id, pair_width)
        key_heads = head_pairs(key_rows, pair_id, pair_width)
        value_heads = head_pairs(value_rows, pair_id, pair_width)
        grad_heads = head_pairs(grad_out, pair_id, pair_width)

        def one_block(carry, items):
            grad_keys, grad_values = carry
            block_id, block_sums = items
            offset = block_id * block_rows
            query_block = lax.dynamic_slice_in_dim(query_heads, offset, block_rows, 0)
            grad_block = lax.dynamic_slice_in_dim(grad_heads, offset, block_rows, 0)
            allowed = allowed_block(offset, block_rows, key_count, key_limit, causal)
            scores = score_block(query_block, key_heads, allowed, score_scale)
            chances = jnp.exp(scores - block_sums[..., None])
            grad_chances = jnp.einsum(
                "qhd,khd->hqk", grad_block, value_heads, preferred_element_type=jnp.float32
            )
            inner = jnp.sum(chances * grad_chances, axis=-1, keepdims=True)
            grad_scores = to_low(chances * (grad_chances - inner))
            grad_query = (
                jnp.einsum(
                    "hqk,khd->qhd", grad_scores, key_heads, preferred_element_type=jnp.float32
                )
                * score_scale
            )
            grad_keys = (
                grad_keys
                + jnp.einsum(
                    "hqk,qhd->khd", grad_scores, query_block, preferred_element_type=jnp.float32
                )
                * score_scale
            )
            grad_values = grad_values + jnp.einsum(
                "hqk,qhd->khd", to_low(chances), grad_block, preferred_element_type=jnp.float32
            )
            return ((grad_keys, grad_values), grad_query.reshape(block_rows, pair_width))

        empty = jnp.zeros((key_count, 2, head_dim), jnp.float32)
        (grad_keys, grad_values), grad_query = lax.scan(
            one_block, (empty, empty), (jnp.arange(length // block_rows), group_sums)
        )
        return (
            grad_query.reshape(length, pair_width),
            grad_keys.reshape(key_count, pair_width),
            grad_values.reshape(key_count, pair_width),
        )

    grad_query, grad_keys, grad_values = lax.map(
        one_group, (jnp.arange(model_width // pair_width), log_sums)
    )
    return (
        grad_query.transpose(1, 0, 2).reshape(length, model_width),
        grad_keys.transpose(1, 0, 2).reshape(key_count, model_width),
        grad_values.transpose(1, 0, 2).reshape(key_count, model_width),
    )


def forward_pass(
    tokens, memory, directions, target_len, memory_len, matrices, vector_rows, ffn_bias
):
    w_qkv, w_out, c_query, c_kv, c_out, f_in, f_out = matrices
    seq_count, length, model_width = tokens.shape
    mem_length = memory.shape[1]
    embedding = jnp.where((directions == 1)[:, None, None], vector_rows[14], vector_rows[13])
    started = (tokens.astype(jnp.float32) + embedding).reshape(seq_count * length, model_width)
    shared = to_low(started)
    projected = product(shared, w_qkv)
    queries = to_low(projected[:, :model_width] + vector_rows[0])
    key_rows = to_low(projected[:, model_width : 2 * model_width])
    value_rows = to_low(projected[:, 2 * model_width :] + vector_rows[1])
    attended, self_sums = lax.map(
        lambda items: attend_forward(items[0], items[1], items[2], items[3], True),
        (
            queries.reshape(seq_count, length, model_width),
            key_rows.reshape(seq_count, length, model_width),
            value_rows.reshape(seq_count, length, model_width),
            target_len,
        ),
    )
    attended = to_low(attended.reshape(-1, model_width))
    first_sum = started + product(attended, w_out) + vector_rows[2]
    first = norm_layer(first_sum, vector_rows[7], vector_rows[10])
    first_low = to_low(first)
    cross_queries = to_low(product(first_low, c_query) + vector_rows[3])
    memory_rows = memory.reshape(seq_count * mem_length, model_width)
    memory_proj = product(memory_rows, c_kv)
    cross_keys = to_low(memory_proj[:, :model_width])
    cross_values = to_low(memory_proj[:, model_width:] + vector_rows[4])
    cross_mixed, cross_sums = lax.map(
        lambda items: attend_forward(items[0], items[1], items[2], items[3], False),
        (
            cross_queries.reshape(seq_count, length, model_width),
            cross_keys.reshape(seq_count, mem_length, model_width),
            cross_values.reshape(seq_count, mem_length, model_width),
            memory_len,
        ),
    )
    cross_mixed = to_low(cross_mixed.reshape(-1, model_width))
    second_sum = first + product(cross_mixed, c_out) + vector_rows[5]
    second = norm_layer(second_sum, vector_rows[8], vector_rows[11])
    second_low = to_low(second)
    hidden_pre = product(second_low, f_in) + ffn_bias
    hidden_act = to_low(gelu_exact(hidden_pre))
    third = second + product(hidden_act, f_out) + vector_rows[6]
    position = lax.iota(jnp.int32, length)
    valid = (position[None, :] < target_len[:, None]).astype(jnp.float32).reshape(-1, 1)
    output = norm_layer(third, vector_rows[9], vector_rows[12]) * valid
    return (
        started,
        shared,
        queries,
        key_rows,
        value_rows,
        self_sums,
        attended,
        first_sum,
        first,
        first_low,
        cross_queries,
        memory_rows,
        cross_keys,
        cross_values,
        cross_sums,
        cross_mixed,
        second_sum,
        second,
        second_low,
        hidden_pre,
        hidden_act,
        third,
        valid,
        output,
    )


def body(
    tokens,
    memory,
    directions,
    target_len,
    memory_len,
    self_qkv,
    self_out,
    cross_query,
    cross_kv,
    cross_out,
    ffn_in,
    ffn_out,
    vectors,
    cotangent,
):
    gathered = (
        lax.all_gather(self_qkv, "dp", axis=0, tiled=True),
        lax.all_gather(self_out, "dp", axis=0, tiled=True),
        lax.all_gather(cross_query, "dp", axis=0, tiled=True),
        lax.all_gather(cross_kv, "dp", axis=0, tiled=True),
        lax.all_gather(cross_out, "dp", axis=0, tiled=True),
        lax.all_gather(ffn_in, "dp", axis=0, tiled=True),
        lax.all_gather(ffn_out, "dp", axis=0, tiled=True),
        lax.all_gather(vectors, "dp", axis=0, tiled=True),
    )
    seq_count, length, model_width = tokens.shape
    mem_length = memory.shape[1]
    ffn_width = gathered[5].shape[0] // model_width
    matrices = (
        gathered[0].reshape(model_width, 3 * model_width),
        gathered[1].reshape(model_width, model_width),
        gathered[2].reshape(model_width, model_width),
        gathered[3].reshape(model_width, 2 * model_width),
        gathered[4].reshape(model_width, model_width),
        gathered[5].reshape(model_width, ffn_width),
        gathered[6].reshape(ffn_width, model_width),
    )
    vector_full = gathered[7].astype(jnp.float32)
    vector_rows = vector_full[: 15 * model_width].reshape(15, model_width)
    ffn_bias = vector_full[15 * model_width :]
    saved = forward_pass(
        tokens, memory, directions, target_len, memory_len, matrices, vector_rows, ffn_bias
    )
    output = saved[-1]
    fresh = lax.optimization_barrier((tokens, memory, matrices, vector_rows, ffn_bias, output))
    saved = forward_pass(
        fresh[0], fresh[1], directions, target_len, memory_len, fresh[2], fresh[3], fresh[4]
    )
    (
        started,
        shared,
        queries,
        key_rows,
        value_rows,
        self_sums,
        attended,
        first_sum,
        first,
        first_low,
        cross_queries,
        memory_rows,
        cross_keys,
        cross_values,
        cross_sums,
        cross_mixed,
        second_sum,
        second,
        second_low,
        hidden_pre,
        hidden_act,
        third,
        valid,
        unused_output,
    ) = saved
    grad_top = cotangent.astype(jnp.float32).reshape(-1, model_width) * valid
    grad_third, grad_gain_three, grad_shift_three = jax.vjp(
        norm_layer, third, vector_rows[9], vector_rows[12]
    )[1](grad_top)
    grad_branch = to_low(grad_third)
    bias_ffn_out = jnp.sum(grad_branch, axis=0, dtype=jnp.float32)
    grad_ffn_out = outer_sum(hidden_act, grad_branch)
    grad_hidden = to_low(
        jax.vjp(gelu_exact, hidden_pre)[1](back_product(grad_branch, matrices[6]))[0]
    )
    bias_ffn_in = jnp.sum(grad_hidden, axis=0, dtype=jnp.float32)
    grad_ffn_in = outer_sum(second_low, grad_hidden)
    grad_second = grad_third + back_product(grad_hidden, matrices[5])
    grad_second_sum, grad_gain_two, grad_shift_two = jax.vjp(
        norm_layer, second_sum, vector_rows[8], vector_rows[11]
    )[1](grad_second)
    grad_cross_branch = to_low(grad_second_sum)
    bias_cross_out = jnp.sum(grad_cross_branch, axis=0, dtype=jnp.float32)
    grad_cross_out = outer_sum(cross_mixed, grad_cross_branch)
    grad_cross_mixed = to_low(back_product(grad_cross_branch, matrices[4]))
    cross_parts = lax.map(
        lambda items: attend_backward(
            items[0], items[1], items[2], items[3], items[4], items[5], False
        ),
        (
            cross_queries.reshape(seq_count, length, model_width),
            cross_keys.reshape(seq_count, mem_length, model_width),
            cross_values.reshape(seq_count, mem_length, model_width),
            cross_sums,
            grad_cross_mixed.reshape(seq_count, length, model_width),
            memory_len,
        ),
    )
    grad_cross_queries = to_low(cross_parts[0].reshape(-1, model_width))
    grad_cross_pair = to_low(
        jnp.concatenate([cross_parts[1], cross_parts[2]], axis=2).reshape(-1, 2 * model_width)
    )
    bias_cross_query = jnp.sum(grad_cross_queries, axis=0, dtype=jnp.float32)
    bias_cross_value = jnp.sum(grad_cross_pair[:, model_width:], axis=0, dtype=jnp.float32)
    grad_cross_query = outer_sum(first_low, grad_cross_queries)
    grad_cross_kv = outer_sum(memory_rows, grad_cross_pair)
    grad_memory = back_product(grad_cross_pair, matrices[3])
    grad_first = grad_second_sum + back_product(grad_cross_queries, matrices[2])
    grad_first_sum, grad_gain_one, grad_shift_one = jax.vjp(
        norm_layer, first_sum, vector_rows[7], vector_rows[10]
    )[1](grad_first)
    grad_self_branch = to_low(grad_first_sum)
    bias_self_out = jnp.sum(grad_self_branch, axis=0, dtype=jnp.float32)
    grad_self_out = outer_sum(attended, grad_self_branch)
    grad_attended = to_low(back_product(grad_self_branch, matrices[1]))
    self_parts = lax.map(
        lambda items: attend_backward(
            items[0], items[1], items[2], items[3], items[4], items[5], True
        ),
        (
            queries.reshape(seq_count, length, model_width),
            key_rows.reshape(seq_count, length, model_width),
            value_rows.reshape(seq_count, length, model_width),
            self_sums,
            grad_attended.reshape(seq_count, length, model_width),
            target_len,
        ),
    )
    grad_projected = to_low(
        jnp.concatenate([self_parts[0], self_parts[1], self_parts[2]], axis=2).reshape(
            -1, 3 * model_width
        )
    )
    bias_query = jnp.sum(grad_projected[:, :model_width], axis=0, dtype=jnp.float32)
    bias_value = jnp.sum(grad_projected[:, 2 * model_width :], axis=0, dtype=jnp.float32)
    grad_self_qkv = outer_sum(shared, grad_projected)
    grad_start = grad_first_sum + back_product(grad_projected, matrices[0])
    per_sequence = jnp.sum(grad_start.reshape(seq_count, length, model_width), axis=1)
    embed_one = jnp.sum(jnp.where((directions == 1)[:, None], per_sequence, 0.0), axis=0)
    embed_zero = jnp.sum(jnp.where((directions == 1)[:, None], 0.0, per_sequence), axis=0)
    grad_vectors = jnp.concatenate(
        [
            jnp.stack(
                [
                    bias_query,
                    bias_value,
                    bias_self_out,
                    bias_cross_query,
                    bias_cross_value,
                    bias_cross_out,
                    bias_ffn_out,
                    grad_gain_one,
                    grad_gain_two,
                    grad_gain_three,
                    grad_shift_one,
                    grad_shift_two,
                    grad_shift_three,
                    embed_zero,
                    embed_one,
                ]
            ).reshape(-1),
            bias_ffn_in,
        ]
    )
    shares = (
        lax.psum_scatter(grad_self_qkv.reshape(-1), "dp", scatter_dimension=0, tiled=True),
        lax.psum_scatter(grad_self_out.reshape(-1), "dp", scatter_dimension=0, tiled=True),
        lax.psum_scatter(grad_cross_query.reshape(-1), "dp", scatter_dimension=0, tiled=True),
        lax.psum_scatter(grad_cross_kv.reshape(-1), "dp", scatter_dimension=0, tiled=True),
        lax.psum_scatter(grad_cross_out.reshape(-1), "dp", scatter_dimension=0, tiled=True),
        lax.psum_scatter(grad_ffn_in.reshape(-1), "dp", scatter_dimension=0, tiled=True),
        lax.psum_scatter(grad_ffn_out.reshape(-1), "dp", scatter_dimension=0, tiled=True),
        lax.psum_scatter(grad_vectors, "dp", scatter_dimension=0, tiled=True),
    )
    return (
        to_low(output).reshape(seq_count, length, model_width),
        grad_start.reshape(seq_count, length, model_width),
        grad_memory.reshape(seq_count, mem_length, model_width),
        shares[0],
        shares[1],
        shares[2],
        shares[3],
        shares[4],
        shares[5],
        shares[6],
        shares[7],
    )


def solution(mesh):
    return jax.shard_map(
        body,
        mesh=mesh,
        in_specs=(
            P("dp", None, None),
            P("dp", None, None),
            P("dp"),
            P("dp"),
            P("dp"),
            P("dp"),
            P("dp"),
            P("dp"),
            P("dp"),
            P("dp"),
            P("dp"),
            P("dp"),
            P("dp"),
            P("dp", None, None),
        ),
        out_specs=(
            P("dp", None, None),
            P("dp", None, None),
            P("dp", None, None),
            P("dp"),
            P("dp"),
            P("dp"),
            P("dp"),
            P("dp"),
            P("dp"),
            P("dp"),
            P("dp"),
        ),
        check_vma=False,
    )
```

profile of v0, /device:TPU:0, one launch (start us, length us, event | category | flops | bytes accessed | tf_op | source)
XLA Modules:
  0.0 1303.5 jit_solution(2763163740462374839)
XLA Ops:
  11.0 42.2 %all-reduce = bf16[9728]{0:T(1024)(128)(2,1)S(1)} all-reduce(bf16[9728]{0:T(1024)(128)(2,1)S(1)} %dynamic-update-slice), channel_id=1, replica_groups=mesh['dp'=32] {'dp'}, use_global_device_ids=true, to_apply=%add | all-reduce | flops 9728 | bytes 38912
  57.4 42.1 %all_gather.26 = bf16[262144]{0:T(1024)(128)(2,1)S(1)} all-gather(bf16[8192]{0:T(1024)(128)(2,1)} %param.44), channel_id=1, replica_groups=mesh['dp'=32] {'dp'}, dimensions={0}, use_global_device_ids=true | all-gather | bytes 540672 | tf_op jit(solution)/shard_map/all_gather | solution.py:262
  100.7 38.2 %all_gather.27 = bf16[262144]{0:T(1024)(128)(2,1)S(1)} all-gather(bf16[8192]{0:T(1024)(128)(2,1)S(1)} %copy-done.92), channel_id=1, replica_groups=mesh['dp'=32] {'dp'}, dimensions={0}, use_global_device_ids=true | all-gather | bytes 540672 | tf_op jit(solution)/shard_map/all_gather | solution.py:263
  140.0 39.9 %all_gather.29 = bf16[262144]{0:T(1024)(128)(2,1)S(1)} all-gather(bf16[8192]{0:T(1024)(128)(2,1)S(1)} %copy-done.93), channel_id=1, replica_groups=mesh['dp'=32] {'dp'}, dimensions={0}, use_global_device_ids=true | all-gather | bytes 540672 | tf_op jit(solution)/shard_map/all_gather | solution.py:265
  200.8 86.2 %while.201 = (s32[]{:T(128)}, bf16[4,1024,128]{1,2,0:T(8,128)(2,1)}, s32[4]{0:T(128)S(1)}, bf16[1024,512]{1,0:T(8,128)(2,1)}, bf16[1024,512]{1,0:T(8,128)(2,1)},...) while((s32[]{:T(128)}, bf16[4,1024,128]{1,2,0:T(8,128)(2,1)}, ...), condition=%wide.region_5.6_spmd, body=%wide.region_0.5_spmd.sunk | while | flops 275252736 | bytes 14955474 | solution.py:95
  292.0 83.6 %while.203 = (s32[]{:T(128)}, bf16[4,1024,128]{1,2,0:T(8,128)(2,1)}, s32[4]{0:T(128)S(1)}, bf16[1024,512]{1,0:T(8,128)(2,1)S(1)}, bf16[1024,512]{1,0:T(8,128)(2,...) while((s32[]{:T(128)}, bf16[4,1024,128]{1,2,0:T(8,128)(2,1)}, ...), condition=%wide.region_13.14_spmd, body=%wide.region_8.13_spmd.sunk | while | flops 274728960 | bytes 13904874 | solution.py:95
  295.2 17.1 %while.213 = (s32[]{:T(128)}, bf16[2,512,128]{2,1,0:T(8,128)(2,1)S(1)}, s32[]{:T(128)}, s32[2]{0:T(128)S(1)}, bf16[1024,2,64]{0,2,1:T(8,128)(2,1)S(1)}, /*index=...) while((s32[]{:T(128)}, ...), condition=%wide.region_12.12_spmd, body=%wide.region_9.11_spmd.sunk | while | flops 274728960 | bytes 9709747 | solution.py:92
  316.0 17.1 %while.213 = (s32[]{:T(128)}, bf16[2,512,128]{2,1,0:T(8,128)(2,1)S(1)}, s32[]{:T(128)}, s32[2]{0:T(128)S(1)}, bf16[1024,2,64]{0,2,1:T(8,128)(2,1)S(1)}, /*index=...) while((s32[]{:T(128)}, ...), condition=%wide.region_12.12_spmd, body=%wide.region_9.11_spmd.sunk | while | flops 274728960 | bytes 9709747 | solution.py:92
  388.9 25.9 %fusion.240 = (f32[1024]{0:T(1024)S(1)}, f32[1024,512]{0,1:T(8,128)S(1)}) fusion(f32[512]{0:T(512)S(1)} %copy-done.129, bf16[2048,512]{1,0:T(8,128)(2,1)} %reshape.742, f32[2048]{0:T(1024)S(1)} %copy-done.101, bf16[512,2048]{1,0:T(8,128)(2,1)} %reshape.741, f32[1024,512]{0,1:T(8,128)} %copy-done.48, f32[512]{0:T(512)S(1)} %copy-done.128, ...), kind=kOutput, calls=%fused_computation.377 | convolution fusion | flops 4439669760 | bytes 8415232 | tf_op jit(solution)/shard_map/dot_general | solution.py:18
  437.9 79.9 %while.205 = (s32[]{:T(128)}, bf16[4,1024,128]{1,2,0:T(8,128)(2,1)}, f32[4,2,2,512]{3,2,1,0:T(2,128)S(1)}, s32[4]{0:T(128)S(1)}, bf16[1024,512]{0,1:T(8,128)(2,1...) while((s32[]{:T(128)}, bf16[4,1024,128]{1,2,0:T(8,128)(2,1)}, ...), condition=%wide.region_23.24_spmd, body=%wide.region_18.23_spmd.sunk | while | flops 281542144 | bytes 19715596 | solution.py:95
  525.2 59.5 %while.207 = (s32[]{:T(128)}, bf16[4,1024,128]{1,2,0:T(8,128)(2,1)}, f32[4,2,2,512]{3,2,1,0:T(2,128)S(1)}, s32[4]{0:T(128)S(1)}, bf16[1024,512]{0,1:T(8,128)(2,1...) while((s32[]{:T(128)}, bf16[4,1024,128]{1,2,0:T(8,128)(2,1)}, ...), condition=%wide.region_31.32_spmd, body=%wide.region_26.31_spmd.sunk | while | flops 281018368 | bytes 17617956 | solution.py:95
  588.3 22.4 %multiply_convert_fusion.2 = (bf16[1024,2048]{1,0:T(8,128)(2,1)S(1)}, f32[1024,2048]{1,0:T(8,128)S(1)}, f32[1024,2048]{1,0:T(8,128)}) fusion(f32[2048]{0:T(1024)S(1)} %copy-done.102, bf16[512,2048]{1,0:T(8,128)(2,1)S(1)} %copy-done.45, f32[1024,512]{0,1:T(8,128)S(1)} %get-tuple-element.1243, f32[512]{0:T(512)S(1)} %bitcast.534, f32[512]{0:T(512)S(1)} %bitcast.537, ...), kind=kOutput, calls=%fused_computation.165 | convolution fusion | flops 2288517120 | bytes 25186304 | tf_op jit(solution)/shard_map/dot_general | solution.py:18
  648.1 156.5 %while.209 = (s32[]{:T(128)}, bf16[4,1024,128]{1,2,0:T(8,128)(2,1)}, bf16[4,1024,128]{1,2,0:T(8,128)(2,1)}, bf16[4,1024,128]{1,2,0:T(8,128)(2,1)}, f32[4,2,2,512...) while((s32[]{:T(128)}, bf16[4,1024,128]{1,2,0:T(8,128)(2,1)}, ...), condition=%wide.region_44.45_spmd, body=%wide.region_40.44_spmd.sunk | while | flops 687603712 | bytes 73059032 | solution.py:156
  652.9 30.5 %while.216 = (s32[]{:T(128)}, f32[1024,2,64]{0,2,1:T(8,128)}, f32[1024,2,64]{0,2,1:T(8,128)}, bf16[2,512,128]{2,1,0:T(8,128)(2,1)}, s32[2]{0:T(128)S(1)}, /*inde...) while((s32[]{:T(128)}, f32[1024,2,64]{0,2,1:T(8,128)}, ...), condition=%wide.region_43.43_spmd.clone, body=%wide.region_41.42_spmd.clone.sunk | while | flops 687603712 | bytes 58623012 | solution.py:147
  692.0 30.5 %while.216 = (s32[]{:T(128)}, f32[1024,2,64]{0,2,1:T(8,128)}, f32[1024,2,64]{0,2,1:T(8,128)}, bf16[2,512,128]{2,1,0:T(8,128)(2,1)}, s32[2]{0:T(128)S(1)}, /*inde...) while((s32[]{:T(128)}, f32[1024,2,64]{0,2,1:T(8,128)}, ...), condition=%wide.region_43.43_spmd.clone, body=%wide.region_41.42_spmd.clone.sunk | while | flops 687603712 | bytes 58623012 | solution.py:147
  731.0 30.5 %while.216 = (s32[]{:T(128)}, f32[1024,2,64]{0,2,1:T(8,128)}, f32[1024,2,64]{0,2,1:T(8,128)}, bf16[2,512,128]{2,1,0:T(8,128)(2,1)}, s32[2]{0:T(128)S(1)}, /*inde...) while((s32[]{:T(128)}, f32[1024,2,64]{0,2,1:T(8,128)}, ...), condition=%wide.region_43.43_spmd.clone, body=%wide.region_41.42_spmd.clone.sunk | while | flops 687603712 | bytes 58623012 | solution.py:147
  770.1 30.5 %while.216 = (s32[]{:T(128)}, f32[1024,2,64]{0,2,1:T(8,128)}, f32[1024,2,64]{0,2,1:T(8,128)}, bf16[2,512,128]{2,1,0:T(8,128)(2,1)}, s32[2]{0:T(128)S(1)}, /*inde...) while((s32[]{:T(128)}, f32[1024,2,64]{0,2,1:T(8,128)}, ...), condition=%wide.region_43.43_spmd.clone, body=%wide.region_41.42_spmd.clone.sunk | while | flops 687603712 | bytes 58623012 | solution.py:147
  819.1 162.8 %while.211 = (s32[]{:T(128)}, bf16[4,1024,128]{1,2,0:T(8,128)(2,1)}, bf16[4,1024,128]{1,2,0:T(8,128)(2,1)}, bf16[4,1024,128]{1,2,0:T(8,128)(2,1)}, f32[4,2,2,512...) while((s32[]{:T(128)}, bf16[4,1024,128]{1,2,0:T(8,128)(2,1)}, ...), condition=%wide.region_51.52_spmd, body=%wide.region_47.51_spmd.sunk | while | flops 688127488 | bytes 79088128 | solution.py:156
  824.5 31.4 %while.217 = (s32[]{:T(128)}, f32[1024,2,64]{0,2,1:T(8,128)}, f32[1024,2,64]{0,2,1:T(8,128)}, bf16[2,512,128]{2,1,0:T(8,128)(2,1)}, s32[2]{0:T(128)S(1)}, /*inde...) while((s32[]{:T(128)}, f32[1024,2,64]{0,2,1:T(8,128)}, ...), condition=%wide.region_50.50_spmd.clone, body=%wide.region_48.49_spmd.clone.sunk | while | flops 688127488 | bytes 64914516 | solution.py:147
  865.1 31.4 %while.217 = (s32[]{:T(128)}, f32[1024,2,64]{0,2,1:T(8,128)}, f32[1024,2,64]{0,2,1:T(8,128)}, bf16[2,512,128]{2,1,0:T(8,128)(2,1)}, s32[2]{0:T(128)S(1)}, /*inde...) while((s32[]{:T(128)}, f32[1024,2,64]{0,2,1:T(8,128)}, ...), condition=%wide.region_50.50_spmd.clone, body=%wide.region_48.49_spmd.clone.sunk | while | flops 688127488 | bytes 64914516 | solution.py:147
  905.7 31.4 %while.217 = (s32[]{:T(128)}, f32[1024,2,64]{0,2,1:T(8,128)}, f32[1024,2,64]{0,2,1:T(8,128)}, bf16[2,512,128]{2,1,0:T(8,128)(2,1)}, s32[2]{0:T(128)S(1)}, /*inde...) while((s32[]{:T(128)}, f32[1024,2,64]{0,2,1:T(8,128)}, ...), condition=%wide.region_50.50_spmd.clone, body=%wide.region_48.49_spmd.clone.sunk | while | flops 688127488 | bytes 64914516 | solution.py:147
  946.2 31.4 %while.217 = (s32[]{:T(128)}, f32[1024,2,64]{0,2,1:T(8,128)}, f32[1024,2,64]{0,2,1:T(8,128)}, bf16[2,512,128]{2,1,0:T(8,128)(2,1)}, s32[2]{0:T(128)S(1)}, /*inde...) while((s32[]{:T(128)}, f32[1024,2,64]{0,2,1:T(8,128)}, ...), condition=%wide.region_50.50_spmd.clone, body=%wide.region_48.49_spmd.clone.sunk | while | flops 688127488 | bytes 64914516 | solution.py:147
  1021.8 39.0 %all-reduce.8 = f32[9728]{0:T(1024)S(1)} all-reduce(f32[9728]{0:T(1024)S(1)} %pad_maximum_fusion.6), channel_id=9, replica_groups=mesh['dp'=32] {'dp'}, use_global_device_ids=true, to_apply=%region_74.75.clone | all-reduce | flops 9728 | bytes 77824
  1066.0 220.4 %all-reduce.12.cloned.1.call-done = (f32[786432]{0:T(1024)}, f32[262144]{0:T(1024)}, f32[262144]{0:T(1024)}, f32[524288]{0:T(1024)}, f32[262144]{0:T(1024)}, /*index=5*/f32[1048576]{0:T(1024)}, f32[1048576]{0:T(1024)}) async-done(((f32[786432]{0:T(1024)}, f32[262144]{0:T(1024)}, f32[262144]{0:T(1024)}, f32[524288]{0:T(1024)}, f32[262144]{0:T(1024)}, /*index=5*/f32[1048576]{0:T(1024)}, f32[1048576]{0:T(1024)}), ...) | async-done | bytes 16777232
  (1487 shorter events, 965.8 us)
Async XLA Ops:
  7.2 178.6 %copy-start = (bf16[1,1024,512]{2,1,0:T(8,128)(2,1)S(1)}, bf16[1,1024,512]{2,1,0:T(8,128)(2,1)}, u32[]{:S(2)}) copy-start(bf16[1,1024,512]{2,1,0:T(8,128)(2,1)} %param.39) | copy-start | bytes 3145732
  7.2 93.5 %copy-start.92 = (bf16[8192]{0:T(1024)(128)(2,1)S(1)}, bf16[8192]{0:T(1024)(128)(2,1)}, u32[]{:S(2)}) copy-start(bf16[8192]{0:T(1024)(128)(2,1)} %param.45) | copy-start | bytes 49156
  7.2 132.8 %copy-start.93 = (bf16[8192]{0:T(1024)(128)(2,1)S(1)}, bf16[8192]{0:T(1024)(128)(2,1)}, u32[]{:S(2)}) copy-start(bf16[8192]{0:T(1024)(128)(2,1)} %param.47) | copy-start | bytes 49156
  7.2 177.0 %all-gather.7.cloned.1.call-start = ((), (), s32[]{:S(2)}) async-start(), calls=%async_computation.1 | async-start | bytes 1081344 | tf_op jit(solution)/shard_map/all_gather | solution.py:264
  7.9 181.5 %all-gather.5.cloned.1.call-start = ((), (), s32[]{:S(2)}) async-start(), calls=%async_computation | async-start | bytes 1622016 | tf_op jit(solution)/shard_map/all_gather | solution.py:261
  8.7 371.6 %all-gather.9.cloned.1.call-start = ((), (), s32[]{:S(2)}) async-start(), calls=%async_computation.2 | async-start | bytes 2162688 | tf_op jit(solution)/shard_map/all_gather | solution.py:266
  9.4 375.1 %all-gather.11.cloned.1.call-start = ((), (), s32[]{:S(2)}) async-start(), calls=%async_computation.3 | async-start | bytes 2162688 | tf_op jit(solution)/shard_map/all_gather | solution.py:267
  10.0 1276.4 %all-reduce.12.cloned.1.call-start = ((), (), s32[]{:S(2)}) async-start(), calls=%async_computation.4 | async-start | bytes 33554432
  55.1 127.8 %copy-start.53 = (bf16[1,1024,512]{2,1,0:T(8,128)(2,1)S(1)}, bf16[1,1024,512]{2,1,0:T(8,128)(2,1)}, u32[]{:S(2)}) copy-start(bf16[1,1024,512]{2,1,0:T(8,128)(2,1)} %param.51) | copy-start | bytes 3145732
  200.7 86.2 %copy-start.62 = (bf16[512,512]{1,0:T(8,128)(2,1)S(1)}, bf16[512,512]{1,0:T(8,128)(2,1)}, u32[]{:S(2)}) copy-start(bf16[512,512]{1,0:T(8,128)(2,1)} %reshape.736) | copy-start | bytes 1572868
  200.8 86.2 %copy-start.127 = (f32[512]{0:T(512)S(1)}, f32[512]{0:T(512)}, u32[]{:S(2)}) copy-start(f32[512]{0:T(512)} %copy-done.126) | copy-start | bytes 6148
  200.8 86.2 %copy-start.134 = (f32[512]{0:T(512)S(1)}, f32[512]{0:T(512)}, u32[]{:S(2)}) copy-start(f32[512]{0:T(512)} %get-tuple-element.1227) | copy-start | bytes 6148
  291.9 83.6 %copy-start.85 = (f32[512]{0:T(512)S(1)}, f32[512]{0:T(512)}, u32[]{:S(2)}) copy-start(f32[512]{0:T(512)} %get-tuple-element.1224) | copy-start | bytes 6148
  291.9 83.6 %copy-start.91 = (f32[1024]{0:T(1024)S(1)}, f32[1024]{0:T(1024)}, u32[]{:S(2)}) copy-start(f32[1024]{0:T(1024)} %copy-done.90) | copy-start | bytes 12292
  291.9 83.6 %copy-start.108 = (f32[1024]{0:T(1024)S(1)}, f32[1024]{0:T(1024)}, u32[]{:S(2)}) copy-start(f32[1024]{0:T(1024)} %copy-done.107) | copy-start | bytes 12292
  292.0 83.6 %copy-start.130 = (f32[512]{0:T(512)S(1)}, f32[512]{0:T(512)}, u32[]{:S(2)}) copy-start(f32[512]{0:T(512)} %get-tuple-element.1222) | copy-start | bytes 6148
  292.0 83.6 %copy-start.132 = (f32[512]{0:T(512)S(1)}, f32[512]{0:T(512)}, u32[]{:S(2)}) copy-start(f32[512]{0:T(512)} %get-tuple-element.1225) | copy-start | bytes 6148
  437.9 79.9 %copy-start.110 = (f32[1,512]{1,0:T(1,128)S(1)}, f32[1,512]{1,0:T(1,128)}, u32[]{:S(2)}) copy-start(f32[1,512]{1,0:T(1,128)} %copy-done.109) | copy-start | bytes 6148
  437.9 79.9 %copy-start.125 = (f32[1,512]{1,0:T(1,128)S(1)}, f32[1,512]{1,0:T(1,128)}, u32[]{:S(2)}) copy-start(f32[1,512]{1,0:T(1,128)} %get-tuple-element.1213) | copy-start | bytes 6148
  525.2 59.5 %copy-start.72 = (f32[1024]{0:T(1024)S(1)}, f32[1024]{0:T(1024)}, u32[]{:S(2)}) copy-start(f32[1024]{0:T(1024)} %copy-done.71) | copy-start | bytes 12292
  525.2 59.5 %copy-start.82 = (f32[1024]{0:T(1024)S(1)}, f32[1024]{0:T(1024)}, u32[]{:S(2)}) copy-start(f32[1024]{0:T(1024)} %copy-done.81) | copy-start | bytes 12292
  525.2 59.5 %copy-start.113 = (f32[1,512]{1,0:T(1,128)S(1)}, f32[1,512]{1,0:T(1,128)}, u32[]{:S(2)}) copy-start(f32[1,512]{1,0:T(1,128)} %get-tuple-element.1211) | copy-start | bytes 6148
  525.2 59.5 %copy-start.116 = (f32[1,512]{1,0:T(1,128)S(1)}, f32[1,512]{1,0:T(1,128)}, u32[]{:S(2)}) copy-start(f32[1,512]{1,0:T(1,128)} %get-tuple-element.1212) | copy-start | bytes 6148
  525.2 59.5 %copy-start.123 = (f32[1,512]{1,0:T(1,128)S(1)}, f32[1,512]{1,0:T(1,128)}, u32[]{:S(2)}) copy-start(f32[1,512]{1,0:T(1,128)} %get-tuple-element.1208) | copy-start | bytes 6148
  (300 other events, 1143.4 us)
Sparse Core Ops, SparseCore 0:
  10.9 56.4 all-gather.6
  70.2 54.5 all-gather.4
  127.7 55.6 all-gather.8
  186.0 55.2 all-gather.10
  1005.4 280.9 all-reduce.11
where the time goes:
time: 1310 us; the launch traced here: 1300 us
  matrix products  431 us (33%)
  local copies, waits for them, and re-layouts  293 us (22%)
  waiting for transfers between devices  223 us (17%)
  blocking collectives  201 us (15%)
  other arithmetic  85.1 us (6%)
  loops' own time  53.2 us (4%)
  between operations  16.9 us (1%)
    unnamed x6, waiting for transfers between devices  223 us
    unnamed x2, blocking collectives  81.2 us
    dot_general x13, matrix products, product(): return jnp.dot(left, right, preferred_element_type=jnp.float32)  76.4 us
    dot_general x32, matrix products, one_block(): jnp.einsum('hqk,khd->qhd', chances, value_heads, preferred_element_type=j...  71.5 us
    dot_general x16, matrix products, one_block(): jnp.einsum('hqk,qhd->khd', to_low(chances), grad_block, preferred_element...  69.8 us
    dynamic_slice x96, local copies, waits for them, and re-layouts, head_pairs(): lax.dynamic_slice_in_dim(matrix, pair_id * pair_width, pair_width, 1)  58.3 us
    sub x16, matrix products, one_block(): powered = jnp.exp(scores - highest)  56.1 us
    dynamic_update_slice x64, local copies, waits for them, and re-layouts, attend_forward(): lax.map(one_group, jnp.arange(model_width // pair_width))  49.5 us
  transfers between devices with their start and end apart: 5, of which 1 were waited for; matrix products, arithmetic and copies ran while one was open for 16% of the time, Pallas kernels for 0%

commit v1 on v0

v1 whole, which is shorter than its diff:
```python
import jax
import jax.numpy as jnp
from jax import lax
from jax.experimental import pallas as pl
from jax.experimental.pallas import tpu as pltpu
from jax.sharding import PartitionSpec as P

HEADS = 8
STEP = 256
PAIR = 2 * STEP
AUG = 16
SAFE_SQUARE = 3600.0
mask_fill = -1000000000.0
norm_eps = 1e-05
low = jnp.bfloat16
full = jnp.float32


def contract(left, right, left_dim, right_dim):
    return lax.dot_general(
        left, right, (((left_dim,), (right_dim,)), ((), ())), preferred_element_type=full
    )


def nn(left, right):
    return contract(left, right, 1, 0)


def tn(left, right):
    return contract(left, right, 0, 0)


def nt(left, right):
    return contract(left, right, 1, 1)


def block(index):
    return slice(index * STEP, (index + 1) * STEP)


def blocks_of(length):
    return (length + STEP - 1) // STEP


def split_three(values):
    first = values.astype(low)
    rest = values - first.astype(full)
    second = rest.astype(low)
    third = (rest - second.astype(full)).astype(low)
    return first, second, third


def normalize(values):
    center = jnp.mean(values, axis=0, keepdims=True)
    offsets = values - center
    spread = jnp.mean(offsets * offsets, axis=0, keepdims=True)
    scale = lax.rsqrt(spread + norm_eps)
    return offsets * scale, scale


def norm_backward(grad, hat, scale, gain):
    scaled = grad * gain
    center = jnp.mean(scaled, axis=0, keepdims=True)
    along = jnp.mean(scaled * hat, axis=0, keepdims=True)
    return (scaled - center - hat * along) * scale


def fold_lanes(values):
    return values[:, :128] + values[:, 128:]


def lane_total(partial):
    ones = jnp.ones((8, 128), full)
    return lax.dot_general(
        ones,
        partial,
        (((1,), (1,)), ((), ())),
        precision=lax.Precision.HIGHEST,
        preferred_element_type=full,
    )[0:1]


def token_total(values):
    return nt(jnp.ones((AUG, values.shape[1]), low), values)[0:1]


def head_rows(head, head_dim):
    return pl.ds(pl.multiple_of(head * head_dim, head_dim), head_dim)


def square_peak(values, head_dim):
    squares = jnp.square(values.astype(full))
    count = values.shape[0] // head_dim
    return jnp.max(jnp.sum(squares.reshape(count, head_dim, values.shape[1]), axis=1))


def attend_forward(q_ref, k_ref, v_ref, mix_ref, sums_ref, mask_rows, head_dim, pairs, keys, shifted):
    causal = mask_rows is None

    def one_head(head, carry):
        rows = head_rows(head, head_dim)
        key_head = k_ref[rows, :keys]
        if not causal:
            key_head = jnp.concatenate([key_head, mask_rows[:, :keys]], 0)
        value_head = jnp.concatenate([v_ref[rows, :keys], jnp.ones((AUG, keys), low)], 0)
        for pair in range(pairs):
            columns = slice(pair * PAIR, (pair + 1) * PAIR)
            query = q_ref[rows, columns]
            if causal:
                main = pair * PAIR + STEP
                scores = tn(key_head[:, :main], query)
                late = tn(key_head[:, main : main + STEP], query[:, STEP:])
                key_pos = lax.broadcasted_iota(jnp.int32, (STEP, STEP), 0)
                query_pos = lax.broadcasted_iota(jnp.int32, (STEP, STEP), 1)
                allowed = key_pos <= query_pos
                edge = scores[main - STEP :]
                edge = jnp.concatenate(
                    [jnp.where(allowed, edge[:, :STEP], mask_fill), edge[:, STEP:]], 1
                )
                scores = edge if main == STEP else jnp.concatenate([scores[: main - STEP], edge], 0)
                late = jnp.where(allowed, late, mask_fill)
            else:
                query = jnp.concatenate([query, jnp.ones((AUG, PAIR), low)], 0)
                scores = tn(key_head, query)
            if shifted:
                highest = jnp.max(scores, axis=0, keepdims=True)
                if causal:
                    second = jnp.maximum(
                        highest[:, STEP:], jnp.max(late, axis=0, keepdims=True)
                    )
                    highest = jnp.concatenate([highest[:, :STEP], second], 1)
                    late = late - second
                scores = scores - highest
            powered = jnp.exp(scores).astype(low)
            if causal:
                mixed = nn(value_head[:, :main], powered)
                extra = nn(value_head[:, main : main + STEP], jnp.exp(late).astype(low))
                mixed = jnp.concatenate([mixed[:, :STEP], mixed[:, STEP:] + extra], 1)
            else:
                mixed = nn(value_head, powered)
            total = mixed[head_dim : head_dim + 1]
            mix_ref[rows, columns] = mixed[:head_dim] / total
            log_sum = jnp.log(total)
            sums_ref[pl.ds(head, 1), columns] = log_sum + highest if shifted else log_sum
        return carry

    lax.fori_loop(0, HEADS, one_head, 0)


def attend_backward(
    q_ref, k_ref, v_ref, mix_ref, sums_ref, grad_ref, dq_ref, dk_ref, dv_ref,
    key_sum, value_sum, mask_rows, head_dim, steps, keys, scale
):
    causal = mask_rows is None
    length = steps * STEP

    def one_head(head, carry):
        rows = head_rows(head, head_dim)
        key_head = k_ref[rows, :keys]
        value_head = v_ref[rows, :keys]
        query = q_ref[rows, :length]
        grad = grad_ref[rows, :length]
        inner = jnp.sum(grad.astype(full) * mix_ref[rows, :length], axis=0, keepdims=True)
        one = jnp.ones((1, length), low)
        blank = jnp.zeros((AUG - 4, length), low)
        query_aug = jnp.concatenate(
            [query, *split_three(sums_ref[pl.ds(head, 1), :length]), one, blank], 0
        )
        grad_aug = jnp.concatenate([grad, *split_three(inner), one, blank], 0)
        minus = jnp.full((3, keys), -1.0, low)
        key_blank = jnp.zeros((AUG - 3, keys), low)
        value_aug = jnp.concatenate([value_head, minus, key_blank], 0)
        if causal:
            key_aug = jnp.concatenate([key_head, minus, key_blank], 0)
        else:
            key_aug = jnp.concatenate(
                [key_head, minus, mask_rows[0:1, :keys], key_blank[1:]], 0
            )
        for step in range(steps):
            span = block(step)
            count = (step + 1) * STEP if causal else keys
            scores = tn(query_aug[:, span], key_aug[:, :count])
            chances = jnp.exp(scores)
            if causal:
                query_pos = lax.broadcasted_iota(jnp.int32, (STEP, STEP), 0)
                key_pos = lax.broadcasted_iota(jnp.int32, (STEP, STEP), 1)
                edge = jnp.where(key_pos <= query_pos, chances[:, count - STEP :], 0.0)
                chances = (
                    edge if count == STEP
                    else jnp.concatenate([chances[:, : count - STEP], edge], 1)
                )
            grad_chances = tn(grad_aug[:, span], value_aug[:, :count])
            grad_scores = (chances * grad_chances).astype(low)
            to_value = nn(grad[:, span], chances.astype(low))
            to_key = nn(query[:, span], grad_scores)
            to_query = nt(key_head[:, :count], grad_scores)
            dq_ref[rows, span] = (to_query * scale).astype(low)
            if step == 0:
                value_sum[:, :count] = to_value
                key_sum[:, :count] = to_key
            elif causal:
                old = count - STEP
                value_sum[:, :old] += to_value[:, :old]
                key_sum[:, :old] += to_key[:, :old]
                value_sum[:, old:count] = to_value[:, old:]
                key_sum[:, old:count] = to_key[:, old:]
            else:
                value_sum[:, :count] += to_value
                key_sum[:, :count] += to_key
        dv_ref[rows, :keys] = value_sum[:, :keys].astype(low)
        dk_ref[rows, :keys] = key_sum[:, :keys].astype(low)
        return carry

    lax.fori_loop(0, HEADS, one_head, 0)


def self_forward_kernel(
    facts, tokens, w_qkv, columns, token_t, q_ref, k_ref, v_ref, mix_ref, sums_ref, peaks
):
    length, width = tokens.shape
    head_dim = width // HEADS
    count = blocks_of(facts[1])
    scale = head_dim ** (-0.5)
    embed = jnp.where(facts[0] == 1, columns[:, 14:15], columns[:, 13:14])
    peaks[0] = 0.0
    peaks[1] = 0.0
    for step in range(length // STEP):

        @pl.when(step < count)
        def project():
            span = block(step)
            flipped = tokens[span, :].T
            token_t[:, span] = flipped
            shared = (flipped.astype(full) + embed).astype(low)
            made = tn(w_qkv[...], shared)
            query = (made[:width] + columns[:, 0:1]).astype(low) * scale
            key = made[width : 2 * width].astype(low)
            q_ref[:, span] = query
            k_ref[:, span] = key
            v_ref[:, span] = (made[2 * width :] + columns[:, 1:2]).astype(low)
            peaks[0] = jnp.maximum(peaks[0], square_peak(query, head_dim))
            peaks[1] = jnp.maximum(peaks[1], square_peak(key, head_dim))

    safe = peaks[0] * peaks[1] <= SAFE_SQUARE
    pairs = (count + 1) // 2
    for wanted in range(1, length // PAIR + 1):
        for shifted in (False, True):

            @pl.when((pairs == wanted) & (safe != shifted))
            def attend():
                attend_forward(
                    q_ref, k_ref, v_ref, mix_ref, sums_ref, None, head_dim, wanted,
                    wanted * PAIR, shifted,
                )


def cross_forward_kernel(
    facts, token_t, memory, mix, w_out, c_query, c_kv, columns,
    hat_ref, scale_ref, memory_t, q_ref, k_ref, v_ref, cross_mix, sums_ref, mask_ref, peaks
):
    length = token_t.shape[1]
    others, width = memory.shape
    head_dim = width // HEADS
    score_scale = head_dim ** (-0.5)
    count = blocks_of(facts[1])
    key_count = blocks_of(facts[2])
    embed = jnp.where(facts[0] == 1, columns[:, 14:15], columns[:, 13:14])
    peaks[0] = 0.0
    peaks[1] = 0.0
    for step in range(others // STEP):

        @pl.when(step < key_count)
        def encode():
            span = block(step)
            flipped = memory[span, :].T
            memory_t[:, span] = flipped
            made = tn(c_kv[...], flipped)
            key = made[:width].astype(low)
            k_ref[:, span] = key
            v_ref[:, span] = (made[width:] + columns[:, 4:5]).astype(low)
            peaks[1] = jnp.maximum(peaks[1], square_peak(key, head_dim))

    for step in range(length // STEP):

        @pl.when(step < count)
        def first():
            span = block(step)
            started = token_t[:, span].astype(full) + embed
            total = started + tn(w_out[...], mix[:, span].astype(low)) + columns[:, 2:3]
            hat, scale = normalize(total)
            hat_ref[:, span] = hat
            scale_ref[:, span] = jnp.broadcast_to(scale, (8, STEP))
            shared = (hat * columns[:, 7:8] + columns[:, 10:11]).astype(low)
            query = (tn(c_query[...], shared) + columns[:, 3:4]).astype(low) * score_scale
            q_ref[:, span] = query
            peaks[0] = jnp.maximum(peaks[0], square_peak(query, head_dim))

    position = lax.broadcasted_iota(jnp.int32, (AUG, others), 1)
    row = lax.broadcasted_iota(jnp.int32, (AUG, others), 0)
    hidden = (position >= facts[2]) & (row == 0)
    mask_ref[...] = jnp.where(hidden, mask_fill, 0.0).astype(low)
    safe = peaks[0] * peaks[1] <= SAFE_SQUARE
    pairs = (count + 1) // 2
    for wanted in range(1, length // PAIR + 1):
        for wanted_keys in range(1, others // STEP + 1):
            for shifted in (False, True):

                @pl.when((pairs == wanted) & (key_count == wanted_keys) & (safe != shifted))
                def attend():
                    attend_forward(
                        q_ref, k_ref, v_ref, cross_mix, sums_ref, mask_ref[...], head_dim,
                        wanted, wanted_keys * STEP, shifted,
                    )


def gelu_parts(values):
    half = 0.5 * (1.0 + lax.erf(values * (0.5**0.5)))
    bell = jnp.exp(-0.5 * values * values) * 0.3989422804014327
    return values * half, half + values * bell


def ffn_kernel(
    facts, hat_one, cross_mix, cotangent, c_out, f_in, f_out, columns,
    out_ref, dr_ref, dmix_ref, g_in, g_out, g_cross_out, g_rows,
    sum_in, sum_out, sum_cross, slope, lanes
):
    length, width = cotangent.shape
    hidden = f_in.shape[1]
    parts = hidden // width
    count = blocks_of(facts[1])
    g_rows[...] = jnp.zeros_like(g_rows)
    lanes[...] = jnp.zeros_like(lanes)
    for step in range(length // STEP):

        @pl.when(step >= count)
        def blank():
            out_ref[block(step), :] = jnp.zeros((STEP, width), low)

        @pl.when(step < count)
        def live():
            span = block(step)

            def gather(ref, value):
                if step == 0:
                    ref[...] = value
                else:
                    ref[...] += value

            mixed = cross_mix[:, span].astype(low)
            first = hat_one[:, span] * columns[:, 7:8] + columns[:, 10:11]
            total = first + tn(c_out[...], mixed) + columns[:, 5:6]
            hat_two, scale_two = normalize(total)
            second = hat_two * columns[:, 8:9] + columns[:, 11:12]
            shared = second.astype(low)
            third = second + columns[:, 6:7]
            acts = []
            for part in range(parts):
                chunk = slice(part * width, (part + 1) * width)
                raw = tn(f_in[:, chunk], shared) + columns[:, 15 + part : 16 + part]
                act, slope_part = gelu_parts(raw)
                slope[chunk, :] = slope_part
                act = act.astype(low)
                acts.append(act)
                third = third + tn(f_out[chunk, :], act)
            hat_three, scale_three = normalize(third)
            position = lax.broadcasted_iota(jnp.int32, (1, STEP), 1) + step * STEP
            valid = (position < facts[1]).astype(full)
            result = (hat_three * columns[:, 9:10] + columns[:, 12:13]) * valid
            out_ref[span, :] = result.astype(low).T
            top = cotangent[span, :].T.astype(full) * valid
            lanes[0] += fold_lanes(top * hat_three)
            lanes[1] += fold_lanes(top)
            grad_third = norm_backward(top, hat_three, scale_three, columns[:, 9:10])
            branch = grad_third.astype(low)
            g_rows[4:5] += token_total(branch)
            grad_second = grad_third
            for part in range(parts):
                chunk = slice(part * width, (part + 1) * width)
                back = nn(f_out[chunk, :], branch)
                gather(sum_out.at[chunk, :], nt(acts[part], branch))
                grad_hidden = (back * slope[chunk, :]).astype(low)
                g_rows[part : part + 1] += token_total(grad_hidden)
                gather(sum_in.at[:, chunk], nt(shared, grad_hidden))
                grad_second = grad_second + nn(f_in[:, chunk], grad_hidden)
            lanes[2] += fold_lanes(grad_second * hat_two)
            lanes[3] += fold_lanes(grad_second)
            grad_two = norm_backward(grad_second, hat_two, scale_two, columns[:, 8:9])
            dr_ref[:, span] = grad_two
            branch_two = grad_two.astype(low)
            g_rows[5:6] += token_total(branch_two)
            gather(sum_cross, nt(mixed, branch_two))
            dmix_ref[:, span] = nn(c_out[...], branch_two).astype(low)

    for index in range(4):
        g_rows[6 + index : 7 + index] = lane_total(lanes[index])
    g_in[...] = sum_in[...].astype(g_in.dtype)
    g_out[...] = sum_out[...].astype(g_out.dtype)
    g_cross_out[...] = sum_cross[...].astype(g_cross_out.dtype)


def cross_backward_kernel(
    facts, q_ref, k_ref, v_ref, cross_mix, sums_ref, dmix, dr_two, hat_one, scale_one, memory_t,
    mix, w_out, c_query, columns,
    dkv_ref, dr_ref, dself, g_query, g_kv, g_out, g_rows,
    dq_ref, key_sum, value_sum, mask_ref, sum_query, sum_kv, sum_out, lanes
):
    width, length = q_ref.shape
    others = k_ref.shape[1]
    head_dim = width // HEADS
    score_scale = head_dim ** (-0.5)
    count = blocks_of(facts[1])
    key_count = blocks_of(facts[2])
    position = lax.broadcasted_iota(jnp.int32, (AUG, others), 1)
    mask_ref[...] = jnp.where(position >= facts[2], mask_fill, 0.0).astype(low)
    for wanted in range(1, length // STEP + 1):
        for wanted_keys in range(1, others // STEP + 1):

            @pl.when((count == wanted) & (key_count == wanted_keys))
            def attend():
                attend_backward(
                    q_ref, k_ref, v_ref, cross_mix, sums_ref, dmix,
                    dq_ref, dkv_ref.at[:width], dkv_ref.at[width:], key_sum, value_sum,
                    mask_ref[...], head_dim, wanted, wanted_keys * STEP, score_scale,
                )

    g_rows[...] = jnp.zeros_like(g_rows)
    lanes[...] = jnp.zeros_like(lanes)
    for step in range(others // STEP):

        @pl.when(step < key_count)
        def encode():
            span = block(step)
            made = nt(memory_t[:, span], dkv_ref[:, span])
            g_rows[1:2] += token_total(dkv_ref[width:, span])
            if step == 0:
                sum_kv[...] = made
            else:
                sum_kv[...] += made

        @pl.when(step >= key_count)
        def blank():
            dkv_ref[:, block(step)] = jnp.zeros((2 * width, STEP), low)

    for step in range(length // STEP):

        @pl.when(step < count)
        def first():
            span = block(step)

            def gather(ref, value):
                if step == 0:
                    ref[...] = value
                else:
                    ref[...] += value

            hat = hat_one[:, span]
            shared = (hat * columns[:, 7:8] + columns[:, 10:11]).astype(low)
            grad_query = dq_ref[:, span]
            g_rows[0:1] += token_total(grad_query)
            gather(sum_query, nt(shared, grad_query))
            grad = dr_two[:, span] + nn(c_query[...], grad_query)
            lanes[0] += fold_lanes(grad * hat)
            lanes[1] += fold_lanes(grad)
            grad_one = norm_backward(grad, hat, scale_one[0:1, span], columns[:, 7:8])
            dr_ref[:, span] = grad_one
            branch = grad_one.astype(low)
            g_rows[2:3] += token_total(branch)
            gather(sum_out, nt(mix[:, span].astype(low), branch))
            dself[:, span] = nn(w_out[...], branch).astype(low)

    g_rows[3:4] = lane_total(lanes[0])
    g_rows[4:5] = lane_total(lanes[1])
    g_query[...] = sum_query[...].astype(g_query.dtype)
    g_kv[...] = sum_kv[...].astype(g_kv.dtype)
    g_out[...] = sum_out[...].astype(g_out.dtype)


def self_backward_kernel(
    facts, token_t, q_ref, k_ref, v_ref, mix, sums_ref, dself, columns,
    grads, g_qkv, g_rows, key_sum, value_sum, sum_qkv
):
    width, length = q_ref.shape
    head_dim = width // HEADS
    score_scale = head_dim ** (-0.5)
    count = blocks_of(facts[1])
    embed = jnp.where(facts[0] == 1, columns[:, 14:15], columns[:, 13:14])
    for wanted in range(1, length // STEP + 1):

        @pl.when(count == wanted)
        def attend():
            attend_backward(
                q_ref, k_ref, v_ref, mix, sums_ref, dself,
                grads.at[:width], grads.at[width : 2 * width], grads.at[2 * width :],
                key_sum, value_sum, None, head_dim, wanted, wanted * STEP, score_scale,
            )

    g_rows[...] = jnp.zeros_like(g_rows)
    for step in range(length // STEP):

        @pl.when(step < count)
        def weights():
            span = block(step)
            shared = (token_t[:, span].astype(full) + embed).astype(low)
            made = nt(shared, grads[:, span])
            g_rows[0:1] += token_total(grads[:width, span])
            g_rows[1:2] += token_total(grads[2 * width :, span])
            if step == 0:
                sum_qkv[...] = made
            else:
                sum_qkv[...] += made

    g_qkv[...] = sum_qkv[...].astype(g_qkv.dtype)


def input_grad_kernel(
    facts, grads, dr_one, w_qkv, dkv, c_kv, d_tokens, d_memory, g_rows, lanes
):
    length, width = d_tokens.shape
    others = d_memory.shape[0]
    count = blocks_of(facts[1])
    key_count = blocks_of(facts[2])
    lanes[...] = jnp.zeros_like(lanes)
    for step in range(length // STEP):

        @pl.when(step < count)
        def live():
            span = block(step)
            made = dr_one[:, span] + nn(w_qkv[...], grads[:, span])
            lanes[...] += fold_lanes(made)
            d_tokens[span, :] = made.T

        @pl.when(step >= count)
        def blank():
            d_tokens[block(step), :] = jnp.zeros((STEP, width), full)

    for step in range(others // STEP):

        @pl.when(step < key_count)
        def encode():
            span = block(step)
            d_memory[span, :] = nn(c_kv[...], dkv[:, span]).T

        @pl.when(step >= key_count)
        def hidden():
            d_memory[block(step), :] = jnp.zeros((STEP, width), full)

    total = lane_total(lanes[...])
    g_rows[...] = jnp.zeros_like(g_rows)
    g_rows[0:1] = jnp.where(facts[0] == 1, 0.0, total)
    g_rows[1:2] = jnp.where(facts[0] == 1, total, 0.0)


def call(kernel, outs, scratch, *args):
    specs = [pl.BlockSpec(memory_space=pltpu.SMEM)]
    specs += [pl.BlockSpec(memory_space=pltpu.VMEM)] * (len(args) - 1)
    return pl.pallas_call(
        kernel,
        out_shape=[jax.ShapeDtypeStruct(shape, dtype) for shape, dtype in outs],
        in_specs=specs,
        out_specs=[pl.BlockSpec(memory_space=pltpu.VMEM)] * len(outs),
        scratch_shapes=scratch,
        compiler_params=pltpu.CompilerParams(vmem_limit_bytes=56 * 2**20),
        name=kernel.__name__,
    )(*args)


def layer(facts, tokens, memory, weights, columns, cotangent, grad_type):
    w_qkv, w_out, c_query, c_kv, c_out, f_in, f_out = weights
    length, width = tokens.shape
    others = memory.shape[0]
    hidden = f_in.shape[1]
    head_dim = width // HEADS
    low_t = ((width, length), low)
    full_t = ((width, length), full)
    sums = ((HEADS, length), full)
    peaks = pltpu.SMEM((2,), full)
    vm = pltpu.VMEM
    token_t, q, k, v, mix, sums_one = call(
        self_forward_kernel, [low_t, low_t, low_t, low_t, full_t, sums], [peaks],
        facts, tokens, w_qkv, columns,
    )
    low_m = ((width, others), low)
    hat, scale, memory_t, cq, ck, cv, cross_mix, sums_two = call(
        cross_forward_kernel,
        [full_t, ((8, length), full), low_m, low_t, low_m, low_m, full_t, sums],
        [vm((AUG, others), low), peaks],
        facts, token_t, memory, mix, w_out, c_query, c_kv, columns,
    )
    out, dr_two, dcross, g_in, g_out, g_cross_out, rows_ffn = call(
        ffn_kernel,
        [((length, width), low), full_t, low_t, ((width, hidden), grad_type),
         ((hidden, width), grad_type), ((width, width), grad_type), ((16, width), full)],
        [vm((width, hidden), full), vm((hidden, width), full), vm((width, width), full),
         vm((hidden, STEP), full), vm((4, width, 128), full)],
        facts, hat, cross_mix, cotangent, c_out, f_in, f_out, columns,
    )
    dkv, dr_one, dself, g_cross_query, g_cross_kv, g_self_out, rows_cross = call(
        cross_backward_kernel,
        [((2 * width, others), low), full_t, low_t, ((width, width), grad_type),
         ((width, 2 * width), grad_type), ((width, width), grad_type), ((8, width), full)],
        [vm((width, length), low), vm((head_dim, others), full), vm((head_dim, others), full),
         vm((AUG, others), low), vm((width, width), full), vm((width, 2 * width), full),
         vm((width, width), full), vm((2, width, 128), full)],
        facts, cq, ck, cv, cross_mix, sums_two, dcross, dr_two, hat, scale, memory_t, mix, w_out,
        c_query, columns,
    )
    grads, g_qkv, rows_self = call(
        self_backward_kernel,
        [((3 * width, length), low), ((width, 3 * width), grad_type), ((8, width), full)],
        [vm((head_dim, length), full), vm((head_dim, length), full), vm((width, 3 * width), full)],
        facts, token_t, q, k, v, mix, sums_one, dself, columns,
    )
    d_tokens, d_memory, rows_input = call(
        input_grad_kernel,
        [((length, width), full), ((others, width), full), ((8, width), full)],
        [vm((width, 128), full)],
        facts, grads, dr_one, w_qkv, dkv, c_kv,
    )
    g_vectors = jnp.concatenate(
        [
            rows_self[0:2],
            rows_cross[2:3],
            rows_cross[0:2],
            rows_ffn[5:6],
            rows_ffn[4:5],
            rows_cross[3:4],
            rows_ffn[8:9],
            rows_ffn[6:7],
            rows_cross[4:5],
            rows_ffn[9:10],
            rows_ffn[7:8],
            rows_input[0:2],
            rows_ffn[0:4],
        ],
        0,
    )
    return (
        out, d_tokens, d_memory,
        (g_qkv, g_self_out, g_cross_query, g_cross_kv, g_cross_out, g_in, g_out), g_vectors,
    )


def body(
    tokens, memory, directions, target_len, memory_len, self_qkv, self_out, cross_query, cross_kv,
    cross_out, ffn_in, ffn_out, vectors, cotangent,
):
    width = tokens.shape[2]
    hidden = (vectors.shape[0] * lax.axis_size("dp")) - 15 * width

    def collect(shard, columns):
        return lax.all_gather(shard.reshape(-1, columns), "dp", axis=0, tiled=True)

    weights = (
        collect(self_qkv, 3 * width),
        collect(self_out, width),
        collect(cross_query, width),
        collect(cross_kv, 2 * width),
        collect(cross_out, width),
        collect(ffn_in, hidden),
        collect(ffn_out, width),
    )
    vector_full = lax.all_gather(vectors, "dp", axis=0, tiled=True).astype(full)
    columns = jnp.pad(vector_full.reshape(-1, width).T, ((0, 0), (0, 109)))
    facts = jnp.concatenate([directions, target_len, memory_len])
    out, d_tokens, d_memory, grads, g_vectors = layer(
        facts, tokens[0], memory[0], weights, columns, cotangent[0], full
    )

    def share(grad):
        return lax.psum_scatter(grad, "dp", scatter_dimension=0, tiled=True).reshape(-1)

    return (
        out[None], d_tokens[None], d_memory[None],
        *[share(grad) for grad in grads],
        share(g_vectors.reshape(-1)),
    )


def solution(mesh):
    rows, flat = P("dp", None, None), P("dp")
    return jax.shard_map(
        body,
        mesh=mesh,
        in_specs=(rows, rows) + (flat,) * 11 + (rows,),
        out_specs=(rows,) * 3 + (flat,) * 8,
        check_vma=False,
    )
```

time: 1310 us -> 1260 us (0.962)
  waiting for transfers between devices: 223 us -> 858 us
  matrix products: 431 us -> 0 us
  local copies, waits for them, and re-layouts: 293 us -> 21.8 us
  Pallas kernels: 0 us -> 102 us
  other arithmetic: 85.1 us -> 1.32 us
  loops' own time: 53.2 us -> 0 us
  blocking collectives: 201 us -> 246 us
    reduce_scatter x0 -> x7, waiting for transfers between devices: none -> 829 us  [share(): lax.psum_scatter(grad, 'dp', scatter_dimension=0, tiled=True).reshape(-1)]
    dot_general x155 -> x0, matrix products: 375 us -> none  [the longest x13 76.4 us: product(): return jnp.dot(left, right, preferred_element_type=jnp.float32)]
    unnamed x6 -> x11, waiting for transfers between devices: 223 us -> 3.21 us
    dynamic_slice x168 -> x0, local copies, waits for them, and re-layouts: 104 us -> none  [the longest x96 58.3 us: head_pairs(): lax.dynamic_slice_in_dim(matrix, pair_id * pair_width, pair_width, 1)]
    pallas_call x0 -> x6, Pallas kernels: none -> 102 us  [call(): pl.pallas_call(kernel, out_shape=[jax.ShapeDtypeStruct(shape, dtype) for...]
    dynamic_update_slice x160 -> x0, local copies, waits for them, and re-layouts: 96.3 us -> none  [the longest x64 49.5 us: attend_forward(): lax.map(one_group, jnp.arange(model_width // pair_width))]
    sub x16 -> x0, matrix products: 56.1 us -> none  [one_block(): powered = jnp.exp(scores - highest)]
    another operation x30 -> x0, loops' own time: 53.2 us -> none  [the longest x16 22 us: one_group(): blended, log_sums = lax.map(one_block, jnp.arange(length // block_rows))]
  transfers between devices with their start and end apart: 5 -> 11, of which waited for: 1 -> 8; matrix products, arithmetic and copies ran while one was open for 16% -> 2% of each run, Pallas kernels for 0% -> 4%
where the time goes in v1:
time: 1260 us; the launch traced here: 1250 us
  waiting for transfers between devices  858 us (68%)
  blocking collectives  246 us (20%)
  Pallas kernels  102 us (8%)
  local copies, waits for them, and re-layouts  21.8 us (2%)
  between operations  16.4 us (1%)
    reduce_scatter x7, waiting for transfers between devices, share(): lax.psum_scatter(grad, 'dp', scatter_dimension=0, tiled=True).reshape(-1)  829 us
    all_gather x3, blocking collectives, collect(): return lax.all_gather(shard.reshape(-1, columns), 'dp', axis=0, tiled=True)  128 us
    unnamed x2, blocking collectives  118 us
    pallas_call x6, Pallas kernels, call(): pl.pallas_call(kernel, out_shape=[jax.ShapeDtypeStruct(shape, dtype) for...  102 us
    all_gather x4, waiting for transfers between devices, collect(): return lax.all_gather(shard.reshape(-1, columns), 'dp', axis=0, tiled=True)  26.1 us
  transfers between devices with their start and end apart: 11, of which 8 were waited for; matrix products, arithmetic and copies ran while one was open for 2% of the time, Pallas kernels for 4%

profile of v1, /device:TPU:0, one launch (start us, length us, event | category | flops | bytes accessed | tf_op | source)
XLA Modules:
  0.0 1246.7 jit_solution(18046605686480704644)
XLA Ops:
  7.2 1.5 reshape.71
  11.8 1.5 reshape.78
  16.3 42.3 %all-reduce.1 = bf16[9728]{0:T(1024)(128)(2,1)S(1)} all-reduce(bf16[9728]{0:T(1024)(128)(2,1)S(1)} %dynamic-update-slice), channel_id=1, replica_groups=mesh['dp'=32] {'dp'}, use_global_device_ids=true, to_apply=%add.1 | all-reduce | flops 9728 | bytes 38912
  62.3 44.5 %all_gather.26.w_out = bf16[512,512]{1,0:T(8,128)(2,1)} all-gather(bf16[16,512]{1,0:T(8,128)(2,1)S(1)} %reshape.73), channel_id=1, replica_groups=mesh['dp'=32] {'dp'}, dimensions={0}, use_global_device_ids=true | all-gather | bytes 540672 | tf_op jit(solution)/shard_map/all_gather | solution.py:651
  106.8 41.1 %all_gather.27.c_query = bf16[512,512]{1,0:T(8,128)(2,1)} all-gather(bf16[16,512]{1,0:T(8,128)(2,1)S(1)} %reshape.74), channel_id=1, replica_groups=mesh['dp'=32] {'dp'}, dimensions={0}, use_global_device_ids=true | all-gather | bytes 540672 | tf_op jit(solution)/shard_map/all_gather | solution.py:651
  147.8 42.7 %all_gather.29.c_out = bf16[512,512]{1,0:T(8,128)(2,1)} all-gather(bf16[16,512]{1,0:T(8,128)(2,1)S(1)} %reshape.76), channel_id=1, replica_groups=mesh['dp'=32] {'dp'}, dimensions={0}, use_global_device_ids=true | all-gather | bytes 540672 | tf_op jit(solution)/shard_map/all_gather | solution.py:651
  190.6 10.5 self_forward_kernel.1
  201.1 17.0 %cross_forward_kernel.1 = (f32[512,1024]{1,0:T(8,128)}, f32[8,1024]{1,0:T(8,128)}, bf16[512,1024]{1,0:T(8,128)(2,1)}, bf16[512,1024]{1,0:T(8,128)(2,1)}, bf16[51...) custom-call(s32[3]{0:T(128)} %pad_add_fusion.facts, ...), custom_call_target="tpu_custom_call" | custom-call | tf_op jit(solution)/shard_map/cross_forward_kernel/pallas_call | solution.py:556
  218.1 26.1 %all-gather.11.cloned.1.call-done.f_out = bf16[2048,512]{1,0:T(8,128)(2,1)} async-done(((bf16[64,512]{1,0:T(8,128)(2,1)}), bf16[2048,512]{1,0:T(8,128)(2,1)}) %all-gather.11.cloned.1.call-update) | async-done | bytes 2097168 | tf_op jit(solution)/shard_map/all_gather | solution.py:651
  244.2 24.5 %ffn_kernel.1 = (bf16[1024,512]{1,0:T(8,128)(2,1)}, f32[512,1024]{1,0:T(8,128)}, bf16[512,1024]{1,0:T(8,128)(2,1)}, f32[512,2048]{1,0:T(8,128)}, f32[2048,512]{1...) custom-call(s32[3]{0:T(128)} %pad_add_fusion.facts, f32[512,1024]{1,0:T(8,128)} %get-tuple-element.47.hat_one, ...), custom_call_target="tpu_custom_call" | custom-call | tf_op jit(solution)/shard_map/ffn_kernel/pallas_call | solution.py:556
  268.7 26.5 %cross_backward_kernel.1 = (bf16[1024,1024]{1,0:T(8,128)(2,1)}, f32[512,1024]{1,0:T(8,128)}, bf16[512,1024]{1,0:T(8,128)(2,1)}, f32[512,512]{1,0:T(8,128)}, f32[...) custom-call(s32[3]{0:T(128)} %pad_add_fusion.facts, bf16[512,1024]{1,0:T(8,128)(2,1)} %get-tuple-element.54.q_ref, ...), custom_call_target="tpu_custom_call" | custom-call | tf_op jit(solution)/shard_map/cross_backward_kernel/pallas_call | solution.py:556
  297.3 14.2 %self_backward_kernel.1 = (bf16[1536,1024]{1,0:T(8,128)(2,1)}, f32[512,1536]{1,0:T(8,128)}, f32[8,512]{1,0:T(8,128)}) custom-call(s32[3]{0:T(128)} %pad_add_fusion.facts, bf16[512,1024]{1,0:T(8,128)(2,1)} %get-tuple-element.45.token_t, bf16[512,1024]{1,0:T(8,128)(2,1)} %get-tuple-element.50.q_ref, bf16[512,1024]{1,0:T(8,128)(2,1)} %get-tuple-element.51.k_ref, ...), custom_call_target="tpu_custom_call" | custom-call | tf_op jit(solution)/shard_map/self_backward_kernel/pallas_call | solution.py:556
  313.6 9.3 input_grad_kernel.1
  323.9 75.7 %all-reduce.2 = f32[9728]{0:T(1024)S(1)} all-reduce(f32[9728]{0:T(1024)S(1)} %reshape.86), channel_id=9, replica_groups=mesh['dp'=32] {'dp'}, use_global_device_ids=true, to_apply=%region_7.8.clone | all-reduce | flops 9728 | bytes 77824
  400.2 52.9 %reduce-scatter.10.cloned.1.call-done = f32[16,512]{1,0:T(8,128)} async-done(((f32[512,512]{1,0:T(8,128)}), f32[16,512]{1,0:T(8,128)}) %reduce-scatter.10.cloned.1.call-update) | async-done | bytes 32784 | tf_op jit(solution)/shard_map/reduce_scatter | solution.py:670
  454.5 132.0 %reduce-scatter.12.cloned.1.call-done = f32[16,512]{1,0:T(8,128)} async-done(((f32[512,512]{1,0:T(8,128)}), f32[16,512]{1,0:T(8,128)}) %reduce-scatter.12.cloned.1.call-update) | async-done | bytes 32784 | tf_op jit(solution)/shard_map/reduce_scatter | solution.py:670
  587.8 132.0 %reduce-scatter.16.cloned.1.call-done = f32[16,512]{1,0:T(8,128)} async-done(((f32[512,512]{1,0:T(8,128)}), f32[16,512]{1,0:T(8,128)}) %reduce-scatter.16.cloned.1.call-update) | async-done | bytes 32784 | tf_op jit(solution)/shard_map/reduce_scatter | solution.py:670
  721.2 133.2 %reduce-scatter.14.cloned.1.call-done = f32[16,1024]{1,0:T(8,128)} async-done(((f32[512,1024]{1,0:T(8,128)}), f32[16,1024]{1,0:T(8,128)}) %reduce-scatter.14.cloned.1.call-update) | async-done | bytes 65552 | tf_op jit(solution)/shard_map/reduce_scatter | solution.py:670
  855.9 101.5 %reduce-scatter.8.cloned.1.call-done = f32[16,1536]{1,0:T(8,128)} async-done(((f32[512,1536]{1,0:T(8,128)}), f32[16,1536]{1,0:T(8,128)}) %reduce-scatter.8.cloned.1.call-update) | async-done | bytes 98320 | tf_op jit(solution)/shard_map/reduce_scatter | solution.py:670
  957.3 1.5 reshape.79
  958.9 140.4 %reduce-scatter.18.cloned.1.call-done = f32[16,2048]{1,0:T(8,128)} async-done(((f32[512,2048]{1,0:T(8,128)}), f32[16,2048]{1,0:T(8,128)}) %reduce-scatter.18.cloned.1.call-update) | async-done | bytes 131088 | tf_op jit(solution)/shard_map/reduce_scatter | solution.py:670
  1099.2 1.6 copy.31
  1100.8 137.3 %reduce-scatter.20.cloned.1.call-done = f32[64,512]{1,0:T(8,128)} async-done(((f32[2048,512]{1,0:T(8,128)}), f32[64,512]{1,0:T(8,128)}) %reduce-scatter.20.cloned.1.call-update) | async-done | bytes 131088 | tf_op jit(solution)/shard_map/reduce_scatter | solution.py:670
  1238.1 1.6 copy.32
  (53 shorter events, 19.1 us)
Async XLA Ops:
  7.2 183.4 %all-gather.5.cloned.1.call-start = ((), (), s32[]{:S(2)}) async-start(), calls=%async_computation.7 | async-start | bytes 1622016 | tf_op jit(solution)/shard_map/all_gather | solution.py:651
  8.8 192.3 %all-gather.7.cloned.1.call-start = ((), (), s32[]{:S(2)}) async-start(), calls=%async_computation.8 | async-start | bytes 1081344 | tf_op jit(solution)/shard_map/all_gather | solution.py:651
  10.2 207.9 %all-gather.9.cloned.1.call-start = ((), (), s32[]{:S(2)}) async-start(), calls=%async_computation.9 | async-start | bytes 2162688 | tf_op jit(solution)/shard_map/all_gather | solution.py:651
  11.8 232.4 %all-gather.11.cloned.1.call-start = ((), (), s32[]{:S(2)}) async-start(), calls=%async_computation.10 | async-start | bytes 2162688 | tf_op jit(solution)/shard_map/all_gather | solution.py:651
  13.4 439.7 %reduce-scatter.10.cloned.1.call-start = ((), (), s32[]{:S(2)}) async-start(), calls=%async_computation.12 | async-start | bytes 1081344 | tf_op jit(solution)/shard_map/reduce_scatter | solution.py:670
  295.2 291.2 %reduce-scatter.12.cloned.1.call-start = ((), (), s32[]{:S(2)}) async-start(), calls=%async_computation.13 | async-start | bytes 1081344 | tf_op jit(solution)/shard_map/reduce_scatter | solution.py:670
  295.8 424.0 %reduce-scatter.16.cloned.1.call-start = ((), (), s32[]{:S(2)}) async-start(), calls=%async_computation.15 | async-start | bytes 1081344 | tf_op jit(solution)/shard_map/reduce_scatter | solution.py:670
  296.5 557.9 %reduce-scatter.14.cloned.1.call-start = ((), (), s32[]{:S(2)}) async-start(), calls=%async_computation.14 | async-start | bytes 2162688 | tf_op jit(solution)/shard_map/reduce_scatter | solution.py:670
  297.3 660.1 %reduce-scatter.8.cloned.1.call-start = ((), (), s32[]{:S(2)}) async-start(), calls=%async_computation.11 | async-start | bytes 3244032 | tf_op jit(solution)/shard_map/reduce_scatter | solution.py:670
  311.5 787.7 %reduce-scatter.18.cloned.1.call-start = ((), (), s32[]{:S(2)}) async-start(), calls=%async_computation.16 | async-start | bytes 4325376 | tf_op jit(solution)/shard_map/reduce_scatter | solution.py:670
  312.1 926.0 %reduce-scatter.20.cloned.1.call-start = ((), (), s32[]{:S(2)}) async-start(), calls=%async_computation.17 | async-start | bytes 4325376 | tf_op jit(solution)/shard_map/reduce_scatter | solution.py:670
  312.2 1.4 copy-start.1
  313.6 10.0 copy-start
Sparse Core Ops, SparseCore 0:
  11.4 57.8 all-gather.4
  72.8 52.6 all-gather.6
  128.9 56.7 all-gather.8
  189.0 55.0 all-gather.10
  295.3 157.6 reduce-scatter.9
  455.3 131.1 reduce-scatter.11
  588.7 131.0 reduce-scatter.15
  722.2 132.2 reduce-scatter.13
  859.8 97.4 reduce-scatter.7
  959.5 139.7 reduce-scatter.17
  1101.5 136.5 reduce-scatter.19
